TPU v7x, 128 devices: a whole 4x4x4 slice. The times are simulated.
128 devices in a mesh: img: 32 (over y, x, z_hi), cen: 4 (over z_lo, core).
Axes of the slice: x: 4, y: 4, z: 4 (z_hi: 2, z_lo: 2; z = z_hi * 2 + z_lo), core: 2. Of those that a mesh axis runs over, the one named last changes fastest.
Arguments:
- embeddings: bfloat16 [32768, 1536], P(('img', 'cen')), may hold values from -8 to 8
- centroids: bfloat16 [4096, 1536], P('cen'), may hold values from -8 to 8
Outputs:
- new_centroids: float32 [4096, 1536], P(('cen', 'img'))
All inputs are finite; a program needn't handle non-finite values.
Results may differ from a plain program's by a relative error of at most 0.0018.
Values may be sent and summed in bfloat16 or wider, within the bound.
A program may use at most 128 MiB of HBM per device.

v0:
```python
import jax
import jax.numpy as jnp
from jax import lax
from jax.sharding import PartitionSpec as P


def from_behind(value, axis, steps):
    count = lax.axis_size(axis)
    pairs = [(source, (source + steps) % count) for source in range(count)]
    return lax.ppermute(value, axis, pairs)


def block_scores(rows, block):
    scale = rows.shape[1] ** (-0.5)
    return (
        lax.dot_general(rows, block, (((1,), (1,)), ((), ())), preferred_element_type=jnp.float32)
        * scale
    )


def full_resp(scores):
    row_max = jnp.max(scores, axis=1, keepdims=True)
    expo = jnp.exp(scores - row_max)
    row_total = jnp.sum(expo, axis=1, keepdims=True)
    return (expo / row_total).astype(jnp.bfloat16)


def weighted_term(resp, rows):
    return lax.dot_general(resp, rows, (((0,), (0,)), ((), ())), preferred_element_type=jnp.float32)


def per_device(embeddings, centroids):
    groups = lax.axis_size("cen")
    position = lax.axis_index("cen")
    kblk = centroids.shape[0]
    rows = embeddings.shape[0]
    block = centroids
    scores = jnp.zeros((rows, groups * kblk), jnp.float32)
    for step in range(groups):
        owner = (position - step) % groups
        scores = lax.dynamic_update_slice_in_dim(
            scores, block_scores(embeddings, block), owner * kblk, 1
        )
        if step + 1 < groups:
            block = from_behind(block, "cen", 1)
    resp = full_resp(scores)
    own_resp = lax.all_to_all(resp, "cen", split_axis=1, concat_axis=0, tiled=True)
    gathered = lax.all_gather(embeddings, "cen", axis=0, tiled=True)
    sums = lax.psum_scatter(
        weighted_term(own_resp, gathered), "img", scatter_dimension=0, tiled=True
    )
    return sums * lax.rsqrt(jnp.mean(sums * sums, axis=1, keepdims=True) + 1e-06)


def solution(mesh):
    placed = (P(("img", "cen"), None), P("cen", None))
    return jax.shard_map(
        per_device, mesh=mesh, in_specs=placed, out_specs=P(("cen", "img"), None), check_vma=False
    )
```

profile of v0, /device:TPU:0, one launch (start us, length us, event | category | flops | bytes accessed | tf_op | source)
XLA Modules:
  0.0 440.6 jit_solution(16576747422683721576)
XLA Ops:
  6.5 0.0 collective-permute-start
  6.5 36.9 %collective-permute-done = bf16[1024,1536]{1,0:T(8,128)(2,1)S(1)} collective-permute-done((bf16[1024,1536]{1,0:T(8,128)(2,1)}, bf16[1024,1536]{1,0:T(8,128)(2,1)S(1)}, u32[]{:S(2)}, u32[]{:S(2)}) %collective-permute-start) | collective-permute-done | bytes 3145760 | tf_op jit(solution)/shard_map/ppermute | solution.py:10
  43.4 1.6 copy-done.1
  45.1 36.8 %collective-permute-done.1 = bf16[1024,1536]{1,0:T(8,128)(2,1)} collective-permute-done((bf16[1024,1536]{1,0:T(8,128)(2,1)S(1)}, bf16[1024,1536]{1,0:T(8,128)(2,1)}, u32[]{:S(2)}, u32[]{:S(2)}) %collective-permute-start.1) | collective-permute-done | bytes 3145760 | tf_op jit(solution)/shard_map/ppermute | solution.py:10
  81.9 0.0 all-gather.2.cloned.1.call-update
  81.9 0.0 reduce-scatter.2.cloned.1.call-start
  82.0 3.2 convolution_multiply_fusion.3
  85.2 0.3 copy.3
  85.6 0.0 copy-start
  85.6 2.4 broadcast_in_dim.2
  88.0 1.1 constant_dynamic-update-slice_fusion.3
  89.0 0.6 copy-done.2
  89.6 1.0 convolution_multiply_fusion.2
  90.6 0.3 copy.4
  90.9 1.1 constant_dynamic-update-slice_fusion.2
  92.0 2.9 convolution_multiply_fusion.1
  94.9 0.3 copy.5
  95.3 1.1 constant_dynamic-update-slice_fusion.1
  96.3 47.8 %collective-permute-done.2 = bf16[1024,1536]{1,0:T(8,128)(2,1)} collective-permute-done((bf16[1024,1536]{1,0:T(8,128)(2,1)}, bf16[1024,1536]{1,0:T(8,128)(2,1)}, u32[]{:S(2)}, u32[]{:S(2)}) %collective-permute-start.2) | collective-permute-done | bytes 3145760 | tf_op jit(solution)/shard_map/ppermute | solution.py:10
  144.2 2.9 convolution_multiply_fusion
  147.1 0.3 copy.6
  147.4 1.0 constant_dynamic-update-slice_fusion
  148.5 2.7 reduce_max.9
  151.2 2.8 fusion
  154.0 2.8 divide_convert_fusion
  156.8 28.8 %all_to_all.19 = bf16[256,4,1024]{0,2,1:T(8,128)(2,1)S(1)} all-to-all(bf16[256,4,1024]{0,2,1:T(8,128)(2,1)S(1)} %bitcast.13), channel_id=1, replica_groups=mesh['img'=32,'cen'=4] {'cen'}, dimensions={1} | all-to-all | bytes 4194304 | tf_op jit(solution)/shard_map/all_to_all | solution.py:47
  185.6 2.5 copy.7
  188.1 8.7 %fusion.1 = f32[1024,1536]{1,0:T(8,128)} fusion(bf16[1024,1024]{1,0:T(8,128)(2,1)} %bitcast.15, bf16[1024,1536]{1,0:T(8,128)(2,1)} %all-gather.2.cloned.1.call-done), kind=kOutput, calls=%fused_computation.14 | convolution fusion | flops 3221225472 | bytes 11534336 | tf_op jit(solution)/shard_map/dot_general | solution.py:29
  196.8 0.0 reduce-scatter.2.cloned.1.call-update
  196.8 234.3 %reduce-scatter.2.cloned.1.call-done = f32[32,1536]{1,0:T(8,128)} async-done(((f32[1024,1536]{1,0:T(8,128)}), f32[32,1536]{1,0:T(8,128)}) %reduce-scatter.2.cloned.1.call-update) | async-done | bytes 196624 | tf_op jit(solution)/shard_map/reduce_scatter | solution.py:49
  431.1 1.0 multiply_reduce_fusion
  432.1 1.7 broadcast_multiply_fusion
  (8 shorter events, 0.0 us)
Async XLA Ops:
  6.5 181.6 %all-gather.2.cloned.1.call-start = ((), (), s32[]{:S(2)}) async-start(), calls=%async_computation.2 | async-start | bytes 3932160 | tf_op jit(solution)/shard_map/all_gather | solution.py:48
  6.5 36.9 %collective-permute-start = (bf16[1024,1536]{1,0:T(8,128)(2,1)}, bf16[1024,1536]{1,0:T(8,128)(2,1)S(1)}, u32[]{:S(2)}, u32[]{:S(2)}) collective-permute-start(bf16[1024,1536]{1,0:T(8,128)(2,1)} %param.3), channel_id=1, source_target_pairs={{0,1},{1,2},{2,3},{3,0},{4,5},{5,6},{6,7},{7,4},{8,9},{9,10},{10,1... | collective-permute-start | bytes 9437192 | tf_op jit(solution)/shard_map/ppermute | solution.py:10
  43.4 1.6 copy-start.1
  45.1 36.8 %collective-permute-start.1 = (bf16[1024,1536]{1,0:T(8,128)(2,1)S(1)}, bf16[1024,1536]{1,0:T(8,128)(2,1)}, u32[]{:S(2)}, u32[]{:S(2)}) collective-permute-start(bf16[1024,1536]{1,0:T(8,128)(2,1)S(1)} %collective-permute-done), channel_id=1, source_target_pairs={{0,1},{1,2},{2,3},{3,0},{4,5},{5,6},{6,7},{7,4},{8,9},{9,10},{10,1... | collective-permute-start | bytes 9437192 | tf_op jit(solution)/shard_map/ppermute | solution.py:10
  81.9 62.3 %collective-permute-start.2 = (bf16[1024,1536]{1,0:T(8,128)(2,1)}, bf16[1024,1536]{1,0:T(8,128)(2,1)}, u32[]{:S(2)}, u32[]{:S(2)}) collective-permute-start(bf16[1024,1536]{1,0:T(8,128)(2,1)} %collective-permute-done.1), channel_id=1, source_target_pairs={{0,1},{1,2},{2,3},{3,0},{4,5},{5,6},{6,7},{7,4},{8,9},{9,10},{10,1... | collective-permute-start | bytes 9437192 | tf_op jit(solution)/shard_map/ppermute | solution.py:10
  81.9 349.1 %reduce-scatter.2.cloned.1.call-start = ((), (), s32[]{:S(2)}) async-start(), calls=%async_computation.3 | async-start | bytes 6488064 | tf_op jit(solution)/shard_map/reduce_scatter | solution.py:49
  85.6 3.5 copy-start
  85.6 4.0 copy-start.2
Sparse Core Ops, SparseCore 0:
  82.0 54.3 all-gather.1
  196.9 234.1 reduce-scatter.1
where the time goes:
time: 441 us
  waiting for transfers between devices  356 us (81%)
  blocking collectives  28.8 us (7%)
  matrix products  18.6 us (4%)
  between operations  13.6 us (3%)
  local copies, waits for them, and re-layouts  12.7 us (3%)
  other arithmetic  11.1 us (3%)
    reduce_scatter x1, waiting for transfers between devices, per_device(): lax.psum_scatter(weighted_term(own_resp, gathered), 'img', scatter_dimens...  234 us
    ppermute x3, waiting for transfers between devices, from_behind(): return lax.ppermute(value, axis, pairs)  122 us
    all_to_all x1, blocking collectives, per_device(): lax.all_to_all(resp, 'cen', split_axis=1, concat_axis=0, tiled=True)  28.8 us
    dot_general x4, matrix products, block_scores(): lax.dot_general(rows, block, (((1,), (1,)), ((), ())), preferred_element_...  9.95 us
  transfers between devices with their start and end apart: 5, of which 4 were waited for; matrix products, arithmetic and copies ran while one was open for 7% of the time, Pallas kernels for 0%

commit v1 on v0

v1 whole, which is shorter than its diff:
```python
import functools
import math

import jax
import jax.numpy as jnp
from jax import lax
from jax.experimental import pallas as pl
from jax.experimental.pallas import tpu as pltpu
from jax.sharding import PartitionSpec as P

MESH = pl.DeviceIdType.MESH
D = 1536
HALF = D // 2
KB = 1024
ROWS = 256
SCALE = D**-0.5 * math.log2(math.e)
WIDTHS = (512, 512, 256, 256)

HOME = 0
NEAR = 2
PASSED = 4
STATS = 6
RING = 8
FAR = 24
N_RECEIVE = 25
ROWS_OUT, STATS_OUT, RING_OUT, FAR_OUT, N_SEND = 0, 1, 2, 10, 11

POWER_SCALE = 2.0**13


def encode(v):
    u = v * POWER_SCALE
    return (u * u * (u * jnp.abs(u))).astype(jnp.bfloat16)


def decode(code):
    c = code.astype(jnp.float32)
    root = lax.rsqrt(lax.rsqrt(jnp.maximum(jnp.abs(c), 2.0**-126))) * (1.0 / POWER_SCALE)
    return jnp.where(c > 0.0, root, jnp.where(c < 0.0, -root, 0.0))


def kernel(e_hbm, c_hbm, out_ref, cen, rows, prob, resp, fac, st, st_in, early, rings, last, lsem, ssem, rsem):
    img, cpos = lax.axis_index("img"), lax.axis_index("cen")
    y, x, zh = lax.div(img, 8), lax.rem(lax.div(img, 2), 4), lax.rem(img, 2)
    zl, core = lax.div(cpos, 2), lax.rem(cpos, 2)
    z = zh * 2 + zl
    other = 1 - core

    def dev(yy, xx, zz, cc):
        return ((yy * 4 + xx) * 2 + lax.div(zz, 2), lax.rem(zz, 2) * 2 + cc)

    def step(v, by):
        return lax.rem(v + by, 4)

    up, down, far = step(z, 1), step(z, 3), step(z, 2)
    sib = dev(y, x, z, other)
    partners = [sib, dev(y, x, far, core)]
    partners += [dev(y, x, zz, cc) for zz in (up, down) for cc in (0, 1)]
    for zz in (z, far):
        partners += [dev(y, step(x, b), zz, core) for b in (1, 2, 3)]
        partners += [dev(step(y, b), x, zz, core) for b in (1, 2, 3)]

    def home(j, cc):
        return rows.at[pl.ds(pl.multiple_of(j * 512 + cc * 128, 128), 128)]

    def outer(j, cc):
        return rows.at[pl.ds(j * 512 + 256, 256), pl.ds(pl.multiple_of(cc * HALF, HALF), HALF)]

    loads = [pltpu.make_async_copy(e_hbm.at[pl.ds(j * 128, 128)], home(j, core), lsem.at[j]) for j in range(2)]
    loads.append(pltpu.make_async_copy(c_hbm, cen, lsem.at[2]))
    for c in loads:
        c.start()

    barrier = pltpu.get_barrier_semaphore()
    for who in partners:
        pl.semaphore_signal(barrier, inc=1, device_id=who, device_id_type=MESH)
    pl.semaphore_wait(barrier, len(partners))

    def copy(src, dst, out, into, who):
        return pltpu.make_async_remote_copy(
            src_ref=src, dst_ref=dst, send_sem=ssem.at[out], recv_sem=rsem.at[into], device_id=who, device_id_type=MESH
        )

    def send(src, dst, out, into, who):
        copy(src, dst, out, into, who).start()

    def arrived(ref, into):
        copy(ref, ref, 0, into, sib).wait_recv()

    def left(ref, out):
        copy(ref, ref, out, 0, sib).wait_send()

    z_to = step(z, 1 + 2 * core)
    for j in range(2):
        half = e_hbm.at[pl.ds(j * 128, 128)]
        for cc in range(2):
            cols = pl.ds(cc * HALF, HALF)
            to = rows.at[pl.ds(pl.multiple_of(j * 512 + 256 + core * 128, 128), 128), cols]
            send(e_hbm.at[pl.ds(j * 128, 128), cols], to, ROWS_OUT, NEAR + j, dev(y, x, z_to, cc))
        send(half, home(j, core), ROWS_OUT, HOME + j, sib)

    def forward(j):
        arrived(outer(j, core), NEAR + j)
        send(outer(j, core), outer(j, core), ROWS_OUT, PASSED + j, sib)

    def dots(ch, first, second):
        chunk = jnp.concatenate([first[...], second[...]], axis=0)
        m = None
        for kt in range(4):
            s = lax.dot_general(
                cen[kt * 256 : kt * 256 + 256, :],
                chunk,
                (((1,), (1,)), ((), ())),
                preferred_element_type=jnp.float32,
            )
            prob[ch, kt * 256 : kt * 256 + 256, :] = s
            top = jnp.max(s, axis=0, keepdims=True)
            m = top if m is None else jnp.maximum(m, top)
        return m

    def exps(ch, m):
        total = jnp.zeros((1, 256), jnp.float32)
        for kt in range(4):
            e = jnp.exp2((prob[ch, kt * 256 : kt * 256 + 256, :] - m) * SCALE)
            prob[ch, kt * 256 : kt * 256 + 256, :] = e
            total = total + jnp.sum(e, axis=0, keepdims=True)
        return total

    def note(j, slot, lanes, m, total):
        st[j, slot, 0:1, :] = m[:, lanes]
        st[j, slot, 1:2, :] = total[:, lanes]

    low, high = slice(0, 128), slice(128, 256)

    def note_home(ch, m, total):
        for j, lanes in enumerate((low, high)):
            note(j, 3 * ch, lanes, m, total)

    def tell(j):
        send(st.at[j], st_in.at[j, 0], STATS_OUT, STATS + j, sib)
        for cc in range(2):
            send(st.at[j, pl.ds(0, 2)], st_in.at[j, 1 + core, pl.ds(2, 2)], STATS_OUT, STATS + j, dev(y, x, up, cc))
            send(st.at[j, pl.ds(2, 2)], st_in.at[j, 1 + core, pl.ds(0, 2)], STATS_OUT, STATS + j, dev(y, x, down, cc))

    for c in loads:
        c.wait()
    m = dots(core, home(0, core), home(1, core))
    note_home(core, m, exps(core, m))
    for j in range(2):
        arrived(home(j, other), HOME + j)
    m = dots(other, home(0, other), home(1, other))
    forward(0)
    note_home(other, m, exps(other, m))
    for j in range(2):
        arrived(outer(j, other), PASSED + j)
        m = dots(2 + j, *(rows.at[j * 512 + 256 + d * 128 : j * 512 + 384 + d * 128] for d in range(2)))
        if j == 0:
            forward(1)
        total = exps(2 + j, m)
        note(j, 2, low, m, total)
        note(j, 1, high, m, total)
        tell(j)

    def respond(j):
        arrived(st_in.at[j], STATS + j)
        for slot, place in enumerate((0, 3, 2, 1)):
            mine = st[j, slot, 0:1, :]
            ms = [mine] + [st_in[j, k, slot, 0:1, :] for k in range(3)]
            ts = [st[j, slot, 1:2, :]] + [st_in[j, k, slot, 1:2, :] for k in range(3)]
            top = functools.reduce(jnp.maximum, ms)
            total = sum(t * jnp.exp2((m - top) * SCALE) for m, t in zip(ms, ts, strict=True))
            lane = j * 512 + place * 128
            fac[0:1, lane : lane + 128] = jnp.exp2((mine - top) * SCALE) / total
        for ch, lanes, at, width in ((0, j * 128, 0, 128), (1, j * 128, 128, 128), (2 + j, 0, 256, 256)):
            cols = slice(j * 512 + at, j * 512 + at + width)
            for kt in range(4):
                ks = slice(kt * 256, kt * 256 + 256)
                resp[ks, cols] = (prob[ch, ks, lanes : lanes + width] * fac[0:1, cols]).astype(jnp.bfloat16)

    def along(axis, by, zz=z):
        return dev(y, step(x, by), zz, core) if axis == 0 else dev(step(y, by), x, zz, core)

    place = (x, y)

    class Ring:
        def __init__(self, number):
            self.number, self.axis, self.width = number, number % 2, WIDTHS[number]
            self.at = sum(WIDTHS[:number])
            self.snd1, self.rcv1, self.next, self.part, self.snd2, self.rcv2 = rings[number]
            self.into, self.out = RING + 4 * number, RING_OUT + 2 * number

        def go1(self, kind, ways=(0, 1)):
            for way in ways:
                into = self.into + (kind > 0)
                send(self.snd1.at[kind, way], self.rcv1.at[kind, way], self.out, into, along(self.axis, 1 + 2 * way))

        def dots(self, by, first=0, last=1024):
            dest = step(place[self.axis], by)
            if self.axis == 0:
                parts = [resp[pl.ds(pl.multiple_of(s * 256 + dest * 64, 64), 64), first:last] for s in range(4)]
                left_side = jnp.concatenate(parts, axis=0)
            else:
                left_side = resp[pl.ds(pl.multiple_of(dest * 256, 256), 256), first:last]
            for c in range(0, self.width, 256):
                end = min(c + 256, self.width)
                right = rows[first:last, self.at + c : self.at + end]
                yield slice(c, end), jnp.dot(left_side, right, preferred_element_type=jnp.float32)

        def early(self, ref):
            for cols, v in self.dots(2, 0, 512):
                ref[:, cols] = v

        def far(self, ref=None):
            for cols, v in self.dots(2) if ref is None else self.dots(2, 512, 1024):
                if ref is not None:
                    v = v + ref[:, cols]
                for s in range(4):
                    for way in range(2):
                        self.snd1[0, way, s, :, cols] = v[s * 64 + way * 32 : s * 64 + way * 32 + 32].astype(jnp.bfloat16)

        def beside(self):
            for way in range(2):
                for cols, v in self.dots(1 + 2 * way):
                    for s in range(4):
                        split = [v[s * 64 + half * 32 : s * 64 + half * 32 + 32] for half in range(2)]
                        self.snd1[1, way, s, :, cols] = split[1 - way].astype(jnp.bfloat16)
                        self.next[way, s, :, cols] = split[way]
                self.go1(1, (way,))

        def own(self):
            for cols, v in self.dots(0):
                for s in range(4):
                    for half in range(2):
                        self.part[s, half, :, cols] = v[s * 64 + half * 32 : s * 64 + half * 32 + 32]

        def relay1(self):
            arrived(self.rcv1.at[0], self.into)
            for way in range(2):
                for s in range(4):
                    v = self.next[way, s] + self.rcv1[0, way, s].astype(jnp.float32)
                    self.snd1[2, way, s] = v.astype(jnp.bfloat16)
                self.go1(2, (way,))

        def arrive1(self):
            arrived(self.rcv1.at[pl.ds(1, 2)], self.into + 1)

        def settled(self, by, half):
            s = step(place[1 - self.axis], by)
            passed, plain = self.rcv1[2, half, s], self.rcv1[1, 1 - half, s]
            return self.part[s, half] + passed.astype(jnp.float32) + plain.astype(jnp.float32)

        def go2(self, way, kind):
            into = self.into + 2 + (kind > 0)
            to = along(1 - self.axis, 1 + 2 * way)
            send(self.snd2.at[way, kind], self.rcv2.at[way, kind], self.out + 1, into, to)

        def out2(self):
            for way in range(2):
                self.snd2[way, 0] = encode(self.settled(2, way))
                self.go2(way, 0)

        def beside2(self):
            for way in range(2):
                self.snd2[way, 1] = encode(self.settled(1 + 2 * way, 1 - way))
                self.go2(way, 1)

        def relay2(self):
            values = [self.settled(1 + 2 * way, way) for way in range(2)]
            arrived(self.rcv2.at[pl.ds(0, 2), 0], self.into + 2)
            for way in range(2):
                self.snd2[way, 2] = encode(values[way] + decode(self.rcv2[way, 0]))
                self.go2(way, 2)

        def out_straight(self):
            for across in (1, 0):
                for by in (2, 1, 3, 0):
                    if by or across:
                        slot = 2 * by + across - 1
                        self.snd2[slot] = encode(self.settled(by, zh + across * (1 - 2 * zh)))
                        to = along(1 - self.axis, by, far if across else z)
                        send(self.snd2.at[slot], self.rcv2.at[slot], self.out + 1, self.into + 2, to)

        def end_straight(self):
            mine = self.settled(0, zh)
            arrived(self.rcv2, self.into + 2)
            out_ref[:, self.at : self.at + self.width] = mine + sum(decode(self.rcv2[slot]) for slot in range(7))

        def end2(self):
            fin, zsnd = last[:2]
            cols = slice(self.at, self.at + self.width)
            values = [self.settled(0, half) for half in range(2)]
            arrived(self.rcv2.at[pl.ds(0, 2), pl.ds(1, 2)], self.into + 3)
            for half in range(2):
                fin[half, :, cols] = values[half] + decode(self.rcv2[half, 2]) + decode(self.rcv2[1 - half, 1])
            zsnd[:, cols] = encode(fin[1 - zh, :, cols])

    def out3():
        send(last[1], last[2], FAR_OUT, FAR, dev(y, x, far, core))

    def end3():
        fin, _, zrcv = last
        arrived(zrcv, FAR)
        out_ref[:, : 2 * WIDTHS[0]] = fin[zh] + decode(zrcv[...])

    a0, b0, a1, b1 = (Ring(n) for n in range(4))

    respond(0)
    a0.early(early.at[0])
    b0.early(early.at[1])
    respond(1)
    a0.far(early.at[0])
    a0.go1(0)
    b0.far(early.at[1])
    b0.go1(0)
    for r in (a0, b0):
        r.beside()
    for r in (a0, b0):
        r.own()
    for r in (a1, b1):
        r.far()
    for r in (a0, b0):
        r.relay1()
    for r in (a1, b1):
        r.go1(0)
    for r in (a1, b1):
        r.beside()
        r.own()
    left(rows.at[pl.ds(0, 768)], ROWS_OUT)
    left(st_in, STATS_OUT)
    for r in (a0, b0):
        r.arrive1()
        r.out2()
    for r in (a1, b1):
        r.relay1()
    for r in (a0, b0):
        r.beside2()
    for r in (a0, b0):
        r.relay2()
    for r in (a1, b1):
        r.arrive1()
        r.out_straight()
    for r in (a0, b0):
        r.end2()
    out3()
    for r in (a0, b0, a1, b1):
        left(r.snd1, r.out)
    for r in (a0, b0):
        left(r.snd2, r.out + 1)
    for r in (a1, b1):
        r.end_straight()
    end3()

    total = out_ref[...]
    norm = lax.rsqrt(jnp.sum(total * total, axis=1, keepdims=True) * (1.0 / D) + 1e-06)
    out_ref[...] = total * norm
    for r in (a1, b1):
        left(r.snd2, r.out + 1)
    left(last[1], FAR_OUT)


def ring_buffers(width):
    f32, bf16 = jnp.float32, jnp.bfloat16
    second = pltpu.VMEM((2, 3, 32, width) if width > 256 else (7, 32, width), bf16)
    return [
        pltpu.VMEM((3, 2, 4, 32, width), bf16),
        pltpu.VMEM((3, 2, 4, 32, width), bf16),
        pltpu.VMEM((2, 4, 32, width), f32),
        pltpu.VMEM((4, 2, 32, width), f32),
        second,
        second,
    ]


def per_device(embeddings, centroids):
    f32, bf16 = jnp.float32, jnp.bfloat16
    return pl.pallas_call(
        kernel,
        out_shape=pltpu.VMEM((32, D), f32),
        in_specs=[pl.BlockSpec(memory_space=pl.ANY)] * 2,
        out_specs=pl.BlockSpec(memory_space=pltpu.VMEM),
        scratch_shapes=[
            pltpu.VMEM((KB, D), bf16),
            pltpu.VMEM((4 * ROWS, D), bf16),
            pltpu.VMEM((4, KB, 256), f32),
            pltpu.VMEM((KB, 4 * ROWS), bf16),
            pltpu.VMEM((8, 4 * ROWS), f32),
            pltpu.VMEM((2, 4, 8, 128), f32),
            pltpu.VMEM((2, 3, 4, 8, 128), f32),
            pltpu.VMEM((2, 256, 512), f32),
            [ring_buffers(width) for width in WIDTHS],
            [
                pltpu.VMEM((2, 32, 2 * WIDTHS[0]), f32),
                pltpu.VMEM((32, 2 * WIDTHS[0]), bf16),
                pltpu.VMEM((32, 2 * WIDTHS[0]), bf16),
            ],
            pltpu.SemaphoreType.DMA((3,)),
            pltpu.SemaphoreType.DMA((N_SEND,)),
            pltpu.SemaphoreType.DMA((N_RECEIVE,)),
        ],
        compiler_params=pltpu.CompilerParams(collective_id=0, has_side_effects=True, vmem_limit_bytes=60 * 1024 * 1024),
        cost_estimate=pl.CostEstimate(flops=4 * KB * 4 * ROWS * D, bytes_accessed=5 * 1024 * 1024, transcendentals=KB * KB),
    )(embeddings, centroids)


def solution(mesh):
    placed = (P(("img", "cen"), None), P("cen", None))
    return jax.shard_map(per_device, mesh=mesh, in_specs=placed, out_specs=P(("cen", "img"), None), check_vma=False)
```

time: 441 us -> 49.4 us (0.11)
  waiting for transfers between devices: 356 us -> 0 us
  Pallas kernels: 0 us -> 48.7 us
  blocking collectives: 28.8 us -> 0 us
  matrix products: 18.6 us -> 0 us
  between operations: 13.6 us -> 0.01 us
  local copies, waits for them, and re-layouts: 12.7 us -> 0.68 us
  other arithmetic: 11.1 us -> 0 us
    reduce_scatter x1 -> x0, waiting for transfers between devices: 234 us -> none  [per_device(): lax.psum_scatter(weighted_term(own_resp, gathered), 'img', scatter_dimens...]
    ppermute x3 -> x0, waiting for transfers between devices: 122 us -> none  [from_behind(): return lax.ppermute(value, axis, pairs)]
    pallas_call x0 -> x1, Pallas kernels: none -> 48.7 us  [per_device(): pl.pallas_call(kernel, out_shape=pltpu.VMEM((32, D), f32), in_specs=[pl.B...]
    all_to_all x1 -> x0, blocking collectives: 28.8 us -> none  [per_device(): lax.all_to_all(resp, 'cen', split_axis=1, concat_axis=0, tiled=True)]
    dot_general x5 -> x0, matrix products: 18.6 us -> none  [the longest x4 9.95 us: block_scores(): lax.dot_general(rows, block, (((1,), (1,)), ((), ())), preferred_element_...]
  transfers between devices with their start and end apart: 5 -> 0, of which waited for: 4 -> 0; matrix products, arithmetic and copies ran while one was open for 7% -> 0% of each run, Pallas kernels for 0% -> 0%
where the time goes in v1:
time: 49.4 us; the launch traced here: 49.3 us
  Pallas kernels  48.7 us (99%)
  local copies, waits for them, and re-layouts  0.68 us (1%)
    pallas_call x1, Pallas kernels, per_device(): pl.pallas_call(kernel, out_shape=pltpu.VMEM((32, D), f32), in_specs=[pl.B...  48.7 us

profile of v1, /device:TPU:0, one launch (start us, length us, event | category | flops | bytes accessed | tf_op | source)
XLA Modules:
  0.0 49.3 jit_solution(16288430628465970748)
XLA Ops:
  0.0 48.7 %shard_map.28 = f32[32,1536]{1,0:T(8,128)S(1)} custom-call(bf16[256,1536]{1,0:T(8,128)(2,1)} %e_hbm.1, bf16[1024,1536]{1,0:T(8,128)(2,1)} %c_hbm.1), custom_call_target="tpu_custom_call" | custom-call | flops 6442450944 | bytes 5242880 | tf_op jit(solution)/shard_map/pallas_call | solution.py:376
  48.7 0.7 %copy.4 = f32[32,1536]{1,0:T(8,128)} copy(f32[32,1536]{1,0:T(8,128)S(1)} %shard_map.28) | data formatting | bytes 393216

commit v2 on v1

--- a/solution.py
+++ b/solution.py
@@ -67,8 +67,9 @@
         return rows.at[pl.ds(j * 512 + 256, 256), pl.ds(pl.multiple_of(cc * HALF, HALF), HALF)]
 
     loads = [pltpu.make_async_copy(e_hbm.at[pl.ds(j * 128, 128)], home(j, core), lsem.at[j]) for j in range(2)]
-    loads.append(pltpu.make_async_copy(c_hbm, cen, lsem.at[2]))
-    for c in loads:
+    quarters = [pl.ds(kt * 256, 256) for kt in range(4)]
+    centroid_loads = [pltpu.make_async_copy(c_hbm.at[at], cen.at[at], lsem.at[2 + kt]) for kt, at in enumerate(quarters)]
+    for c in loads + centroid_loads:
         c.start()
 
     barrier = pltpu.get_barrier_semaphore()
@@ -103,10 +104,12 @@
         arrived(outer(j, core), NEAR + j)
         send(outer(j, core), outer(j, core), ROWS_OUT, PASSED + j, sib)
 
-    def dots(ch, first, second):
+    def dots(ch, first, second, waits=()):
         chunk = jnp.concatenate([first[...], second[...]], axis=0)
         m = None
         for kt in range(4):
+            if waits:
+                waits[kt].wait()
             s = lax.dot_general(
                 cen[kt * 256 : kt * 256 + 256, :],
                 chunk,
@@ -144,7 +147,7 @@
 
     for c in loads:
         c.wait()
-    m = dots(core, home(0, core), home(1, core))
+    m = dots(core, home(0, core), home(1, core), centroid_loads)
     note_home(core, m, exps(core, m))
     for j in range(2):
         arrived(home(j, other), HOME + j)
@@ -393,7 +396,7 @@
                 pltpu.VMEM((32, 2 * WIDTHS[0]), bf16),
                 pltpu.VMEM((32, 2 * WIDTHS[0]), bf16),
             ],
-            pltpu.SemaphoreType.DMA((3,)),
+            pltpu.SemaphoreType.DMA((6,)),
             pltpu.SemaphoreType.DMA((N_SEND,)),
             pltpu.SemaphoreType.DMA((N_RECEIVE,)),
         ],

time: 49.4 us -> 49.5 us (level)
  no operation moved by 1% of the time
where the time goes in v2:
time: 49.5 us; the launch traced here: 49.4 us
  Pallas kernels  48.7 us (98%)
  local copies, waits for them, and re-layouts  0.68 us (1%)
    pallas_call x1, Pallas kernels, per_device(): pl.pallas_call(kernel, out_shape=pltpu.VMEM((32, D), f32), in_specs=[pl.B...  48.7 us

profile of v2, /device:TPU:0, one launch (start us, length us, event | category | flops | bytes accessed | tf_op | source)
XLA Modules:
  0.0 49.4 jit_solution(8898139684324472992)
XLA Ops:
  0.0 48.7 %shard_map.28 = f32[32,1536]{1,0:T(8,128)S(1)} custom-call(bf16[256,1536]{1,0:T(8,128)(2,1)} %e_hbm.1, bf16[1024,1536]{1,0:T(8,128)(2,1)} %c_hbm.1), custom_call_target="tpu_custom_call" | custom-call | flops 6442450944 | bytes 5242880 | tf_op jit(solution)/shard_map/pallas_call | solution.py:379
  48.7 0.7 %copy.4 = f32[32,1536]{1,0:T(8,128)} copy(f32[32,1536]{1,0:T(8,128)S(1)} %shard_map.28) | data formatting | bytes 393216

commit v3 on v1

--- a/solution.py
+++ b/solution.py
@@ -14,6 +14,7 @@
 KB = 1024
 ROWS = 256
 SCALE = D**-0.5 * math.log2(math.e)
+SPLIT = (128, 96)
 WIDTHS = (512, 512, 256, 256)
 
 HOME = 0
@@ -22,7 +23,8 @@
 STATS = 6
 RING = 8
 FAR = 24
-N_RECEIVE = 25
+BOTH = 25
+N_RECEIVE = 26
 ROWS_OUT, STATS_OUT, RING_OUT, FAR_OUT, N_SEND = 0, 1, 2, 10, 11
 
 POWER_SCALE = 2.0**13
@@ -61,10 +63,13 @@
         partners += [dev(step(y, b), x, zz, core) for b in (1, 2, 3)]
 
     def home(j, cc):
-        return rows.at[pl.ds(pl.multiple_of(j * 512 + cc * 128, 128), 128)]
+        return rows.at[j * 4 + cc]
+
+    def columns(cc):
+        return pl.ds(pl.multiple_of(cc * HALF, HALF), HALF)
 
     def outer(j, cc):
-        return rows.at[pl.ds(j * 512 + 256, 256), pl.ds(pl.multiple_of(cc * HALF, HALF), HALF)]
+        return rows.at[pl.ds(j * 4 + 2, 2), pl.ds(0, SPLIT[j]), columns(cc)]
 
     loads = [pltpu.make_async_copy(e_hbm.at[pl.ds(j * 128, 128)], home(j, core), lsem.at[j]) for j in range(2)]
     loads.append(pltpu.make_async_copy(c_hbm, cen, lsem.at[2]))
@@ -92,12 +97,14 @@
 
     z_to = step(z, 1 + 2 * core)
     for j in range(2):
-        half = e_hbm.at[pl.ds(j * 128, 128)]
         for cc in range(2):
-            cols = pl.ds(cc * HALF, HALF)
-            to = rows.at[pl.ds(pl.multiple_of(j * 512 + 256 + core * 128, 128), 128), cols]
-            send(e_hbm.at[pl.ds(j * 128, 128), cols], to, ROWS_OUT, NEAR + j, dev(y, x, z_to, cc))
-        send(half, home(j, core), ROWS_OUT, HOME + j, sib)
+            src = e_hbm.at[pl.ds(j * 128, SPLIT[j]), columns(cc)]
+            send(src, rows.at[j * 4 + 2 + core, pl.ds(0, SPLIT[j]), columns(cc)], ROWS_OUT, NEAR + j, dev(y, x, z_to, cc))
+        send(e_hbm.at[pl.ds(j * 128, 128)], home(j, core), ROWS_OUT, HOME + j, sib)
+    tail = pl.ds(SPLIT[1], 128 - SPLIT[1])
+    for cc in range(2):
+        src = e_hbm.at[pl.ds(128 + SPLIT[1], 128 - SPLIT[1])]
+        send(src, rows.at[6 + core, tail], ROWS_OUT, BOTH, dev(y, x, z_to, cc))
 
     def forward(j):
         arrived(outer(j, core), NEAR + j)
@@ -153,7 +160,9 @@
     note_home(other, m, exps(other, m))
     for j in range(2):
         arrived(outer(j, other), PASSED + j)
-        m = dots(2 + j, *(rows.at[j * 512 + 256 + d * 128 : j * 512 + 384 + d * 128] for d in range(2)))
+        if j == 1:
+            arrived(rows.at[pl.ds(6, 2), tail], BOTH)
+        m = dots(2 + j, rows.at[j * 4 + 2], rows.at[j * 4 + 3])
         if j == 0:
             forward(1)
         total = exps(2 + j, m)
@@ -203,7 +212,7 @@
                 left_side = resp[pl.ds(pl.multiple_of(dest * 256, 256), 256), first:last]
             for c in range(0, self.width, 256):
                 end = min(c + 256, self.width)
-                right = rows[first:last, self.at + c : self.at + end]
+                right = rows[first // 128 : last // 128, :, self.at + c : self.at + end].reshape(last - first, end - c)
                 yield slice(c, end), jnp.dot(left_side, right, preferred_element_type=jnp.float32)
 
         def early(self, ref):
@@ -325,7 +334,7 @@
     for r in (a1, b1):
         r.beside()
         r.own()
-    left(rows.at[pl.ds(0, 768)], ROWS_OUT)
+    left(rows.at[pl.ds(0, 6)], ROWS_OUT)
     left(st_in, STATS_OUT)
     for r in (a0, b0):
         r.arrive1()
@@ -380,7 +389,7 @@
         out_specs=pl.BlockSpec(memory_space=pltpu.VMEM),
         scratch_shapes=[
             pltpu.VMEM((KB, D), bf16),
-            pltpu.VMEM((4 * ROWS, D), bf16),
+            pltpu.VMEM((8, 128, D), bf16),
             pltpu.VMEM((4, KB, 256), f32),
             pltpu.VMEM((KB, 4 * ROWS), bf16),
             pltpu.VMEM((8, 4 * ROWS), f32),

time: 49.4 us -> 48.8 us (0.988)
  Pallas kernels: 48.7 us -> 48 us
    pallas_call x1, Pallas kernels: 48.7 us -> 48 us  [per_device(): pl.pallas_call(kernel, out_shape=pltpu.VMEM((32, D), f32), in_specs=[pl.B...]
where the time goes in v3:
time: 48.8 us; the launch traced here: 48.7 us
  Pallas kernels  48 us (98%)
  local copies, waits for them, and re-layouts  0.68 us (1%)
    pallas_call x1, Pallas kernels, per_device(): pl.pallas_call(kernel, out_shape=pltpu.VMEM((32, D), f32), in_specs=[pl.B...  48 us

profile of v3, /device:TPU:0, one launch (start us, length us, event | category | flops | bytes accessed | tf_op | source)
XLA Modules:
  0.0 48.7 jit_solution(8838506025503418415)
XLA Ops:
  0.0 48.0 %shard_map.28 = f32[32,1536]{1,0:T(8,128)S(1)} custom-call(bf16[256,1536]{1,0:T(8,128)(2,1)} %e_hbm.1, bf16[1024,1536]{1,0:T(8,128)(2,1)} %c_hbm.1), custom_call_target="tpu_custom_call" | custom-call | flops 6442450944 | bytes 5242880 | tf_op jit(solution)/shard_map/pallas_call | solution.py:385
  48.0 0.7 %copy.4 = f32[32,1536]{1,0:T(8,128)} copy(f32[32,1536]{1,0:T(8,128)S(1)} %shard_map.28) | data formatting | bytes 393216

commit v4 on v3

--- a/solution.py
+++ b/solution.py
@@ -56,11 +56,9 @@
 
     up, down, far = step(z, 1), step(z, 3), step(z, 2)
     sib = dev(y, x, z, other)
-    partners = [sib, dev(y, x, far, core)]
-    partners += [dev(y, x, zz, cc) for zz in (up, down) for cc in (0, 1)]
-    for zz in (z, far):
-        partners += [dev(y, step(x, b), zz, core) for b in (1, 2, 3)]
-        partners += [dev(step(y, b), x, zz, core) for b in (1, 2, 3)]
+    partners = [dev(y, x, zz, cc) for zz in (up, down) for cc in (0, 1)] + [sib]
+    partners += [dev(y, step(x, b), z, core) for b in (1, 3)]
+    partners += [dev(step(y, b), x, z, core) for b in (1, 3)]
 
     def home(j, cc):
         return rows.at[j * 4 + cc]
@@ -144,10 +142,10 @@
             note(j, 3 * ch, lanes, m, total)
 
     def tell(j):
-        send(st.at[j], st_in.at[j, 0], STATS_OUT, STATS + j, sib)
         for cc in range(2):
             send(st.at[j, pl.ds(0, 2)], st_in.at[j, 1 + core, pl.ds(2, 2)], STATS_OUT, STATS + j, dev(y, x, up, cc))
             send(st.at[j, pl.ds(2, 2)], st_in.at[j, 1 + core, pl.ds(0, 2)], STATS_OUT, STATS + j, dev(y, x, down, cc))
+        send(st.at[j], st_in.at[j, 0], STATS_OUT, STATS + j, sib)
 
     for c in loads:
         c.wait()

time: 48.8 us -> 47.8 us (0.980)
  Pallas kernels: 48 us -> 47 us
    pallas_call x1, Pallas kernels: 48 us -> 47 us  [per_device(): pl.pallas_call(kernel, out_shape=pltpu.VMEM((32, D), f32), in_specs=[pl.B...]
where the time goes in v4:
time: 47.8 us; the launch traced here: 47.7 us
  Pallas kernels  47 us (98%)
  local copies, waits for them, and re-layouts  0.68 us (1%)
    pallas_call x1, Pallas kernels, per_device(): pl.pallas_call(kernel, out_shape=pltpu.VMEM((32, D), f32), in_specs=[pl.B...  47 us

profile of v4, /device:TPU:0, one launch (start us, length us, event | category | flops | bytes accessed | tf_op | source)
XLA Modules:
  0.0 47.7 jit_solution(4259101160937426835)
XLA Ops:
  0.0 47.0 %shard_map.28 = f32[32,1536]{1,0:T(8,128)S(1)} custom-call(bf16[256,1536]{1,0:T(8,128)(2,1)} %e_hbm.1, bf16[1024,1536]{1,0:T(8,128)(2,1)} %c_hbm.1), custom_call_target="tpu_custom_call" | custom-call | flops 6442450944 | bytes 5242880 | tf_op jit(solution)/shard_map/pallas_call | solution.py:383
  47.0 0.7 %copy.4 = f32[32,1536]{1,0:T(8,128)} copy(f32[32,1536]{1,0:T(8,128)S(1)} %shard_map.28) | data formatting | bytes 393216

commit v5 on v4

--- a/solution.py
+++ b/solution.py
@@ -60,6 +60,10 @@
     partners += [dev(y, step(x, b), z, core) for b in (1, 3)]
     partners += [dev(step(y, b), x, z, core) for b in (1, 3)]
 
+    barrier = pltpu.get_barrier_semaphore()
+    for who in partners:
+        pl.semaphore_signal(barrier, inc=1, device_id=who, device_id_type=MESH)
+
     def home(j, cc):
         return rows.at[j * 4 + cc]
 
@@ -74,9 +78,6 @@
     for c in loads:
         c.start()
 
-    barrier = pltpu.get_barrier_semaphore()
-    for who in partners:
-        pl.semaphore_signal(barrier, inc=1, device_id=who, device_id_type=MESH)
     pl.semaphore_wait(barrier, len(partners))
 
     def copy(src, dst, out, into, who):
@@ -98,7 +99,9 @@
         for cc in range(2):
             src = e_hbm.at[pl.ds(j * 128, SPLIT[j]), columns(cc)]
             send(src, rows.at[j * 4 + 2 + core, pl.ds(0, SPLIT[j]), columns(cc)], ROWS_OUT, NEAR + j, dev(y, x, z_to, cc))
-        send(e_hbm.at[pl.ds(j * 128, 128)], home(j, core), ROWS_OUT, HOME + j, sib)
+        if j == 0:
+            for half in range(2):
+                send(e_hbm.at[pl.ds(half * 128, 128)], home(half, core), ROWS_OUT, HOME + half, sib)
     tail = pl.ds(SPLIT[1], 128 - SPLIT[1])
     for cc in range(2):
         src = e_hbm.at[pl.ds(128 + SPLIT[1], 128 - SPLIT[1])]

time: 47.8 us -> 47.8 us (level)
  no operation moved by 1% of the time
where the time goes in v5:
time: 47.8 us; the launch traced here: 47.7 us
  Pallas kernels  47 us (98%)
  local copies, waits for them, and re-layouts  0.68 us (1%)
    pallas_call x1, Pallas kernels, per_device(): pl.pallas_call(kernel, out_shape=pltpu.VMEM((32, D), f32), in_specs=[pl.B...  47 us

profile of v5, /device:TPU:0, one launch (start us, length us, event | category | flops | bytes accessed | tf_op | source)
XLA Modules:
  0.0 47.7 jit_solution(15009828611348740805)
XLA Ops:
  0.0 47.0 %shard_map.28 = f32[32,1536]{1,0:T(8,128)S(1)} custom-call(bf16[256,1536]{1,0:T(8,128)(2,1)} %e_hbm.1, bf16[1024,1536]{1,0:T(8,128)(2,1)} %c_hbm.1), custom_call_target="tpu_custom_call" | custom-call | flops 6442450944 | bytes 5242880 | tf_op jit(solution)/shard_map/pallas_call | solution.py:386
  47.0 0.7 %copy.4 = f32[32,1536]{1,0:T(8,128)} copy(f32[32,1536]{1,0:T(8,128)S(1)} %shard_map.28) | data formatting | bytes 393216

commit v6 on v4

--- a/solution.py
+++ b/solution.py
@@ -22,10 +22,9 @@
 PASSED = 4
 STATS = 6
 RING = 8
-FAR = 24
-BOTH = 25
-N_RECEIVE = 26
-ROWS_OUT, STATS_OUT, RING_OUT, FAR_OUT, N_SEND = 0, 1, 2, 10, 11
+BOTH = 24
+N_RECEIVE = 25
+ROWS_OUT, STATS_OUT, RING_OUT, N_SEND = 0, 1, 2, 10
 
 POWER_SCALE = 2.0**13
 
@@ -41,7 +40,7 @@
     return jnp.where(c > 0.0, root, jnp.where(c < 0.0, -root, 0.0))
 
 
-def kernel(e_hbm, c_hbm, out_ref, cen, rows, prob, resp, fac, st, st_in, early, rings, last, lsem, ssem, rsem):
+def kernel(e_hbm, c_hbm, out_ref, cen, rows, prob, resp, fac, st, st_in, early, rings, lsem, ssem, rsem):
     img, cpos = lax.axis_index("img"), lax.axis_index("cen")
     y, x, zh = lax.div(img, 8), lax.rem(lax.div(img, 2), 4), lax.rem(img, 2)
     zl, core = lax.div(cpos, 2), lax.rem(cpos, 2)
@@ -256,27 +255,36 @@
             passed, plain = self.rcv1[2, half, s], self.rcv1[1, 1 - half, s]
             return self.part[s, half] + passed.astype(jnp.float32) + plain.astype(jnp.float32)
 
-        def go2(self, way, kind):
-            into = self.into + 2 + (kind > 0)
-            to = along(1 - self.axis, 1 + 2 * way)
-            send(self.snd2.at[way, kind], self.rcv2.at[way, kind], self.out + 1, into, to)
-
         def out2(self):
             for way in range(2):
-                self.snd2[way, 0] = encode(self.settled(2, way))
-                self.go2(way, 0)
+                self.snd2[way] = encode(self.settled(2, way))
+                to = along(1 - self.axis, 1 + 2 * way)
+                send(self.snd2.at[way], self.rcv2.at[way], self.out + 1, self.into + 2, to)
+
+        def go2(self, way, kind, half):
+            across = (half - zh) * (half - zh)
+            to = along(1 - self.axis, 1 + 2 * way, step(z, 2 * across))
+            src = self.snd2.at[2 * kind + way]
+            send(src, self.rcv2.at[2 * kind + across], self.out + 1, self.into + 3, to)
 
         def beside2(self):
             for way in range(2):
-                self.snd2[way, 1] = encode(self.settled(1 + 2 * way, 1 - way))
-                self.go2(way, 1)
+                self.snd2[2 + way] = encode(self.settled(1 + 2 * way, 1 - way))
+                self.go2(way, 1, 1 - way)
+            self.snd2[6] = encode(self.settled(0, 1 - zh))
+            send(self.snd2.at[6], self.rcv2.at[6], self.out + 1, self.into + 3, dev(y, x, far, core))
 
         def relay2(self):
             values = [self.settled(1 + 2 * way, way) for way in range(2)]
-            arrived(self.rcv2.at[pl.ds(0, 2), 0], self.into + 2)
-            for way in range(2):
-                self.snd2[way, 2] = encode(values[way] + decode(self.rcv2[way, 0]))
-                self.go2(way, 2)
+            arrived(self.rcv2.at[pl.ds(0, 2)], self.into + 2)
+            for way in range(2):
+                self.snd2[4 + way] = encode(values[way] + decode(self.rcv2[way]))
+                self.go2(way, 2, way)
+
+        def end2(self):
+            mine = self.settled(0, zh)
+            arrived(self.rcv2.at[pl.ds(2, 5)], self.into + 3)
+            out_ref[:, self.at : self.at + self.width] = mine + sum(decode(self.rcv2[slot]) for slot in range(2, 7))
 
         def out_straight(self):
             for across in (1, 0):
@@ -292,23 +300,6 @@
             arrived(self.rcv2, self.into + 2)
             out_ref[:, self.at : self.at + self.width] = mine + sum(decode(self.rcv2[slot]) for slot in range(7))
 
-        def end2(self):
-            fin, zsnd = last[:2]
-            cols = slice(self.at, self.at + self.width)
-            values = [self.settled(0, half) for half in range(2)]
-            arrived(self.rcv2.at[pl.ds(0, 2), pl.ds(1, 2)], self.into + 3)
-            for half in range(2):
-                fin[half, :, cols] = values[half] + decode(self.rcv2[half, 2]) + decode(self.rcv2[1 - half, 1])
-            zsnd[:, cols] = encode(fin[1 - zh, :, cols])
-
-    def out3():
-        send(last[1], last[2], FAR_OUT, FAR, dev(y, x, far, core))
-
-    def end3():
-        fin, _, zrcv = last
-        arrived(zrcv, FAR)
-        out_ref[:, : 2 * WIDTHS[0]] = fin[zh] + decode(zrcv[...])
-
     a0, b0, a1, b1 = (Ring(n) for n in range(4))
 
     respond(0)
@@ -346,28 +337,25 @@
     for r in (a1, b1):
         r.arrive1()
         r.out_straight()
-    for r in (a0, b0):
-        r.end2()
-    out3()
     for r in (a0, b0, a1, b1):
         left(r.snd1, r.out)
     for r in (a0, b0):
         left(r.snd2, r.out + 1)
+    for r in (a0, b0):
+        r.end2()
     for r in (a1, b1):
         r.end_straight()
-    end3()
 
     total = out_ref[...]
     norm = lax.rsqrt(jnp.sum(total * total, axis=1, keepdims=True) * (1.0 / D) + 1e-06)
     out_ref[...] = total * norm
     for r in (a1, b1):
         left(r.snd2, r.out + 1)
-    left(last[1], FAR_OUT)
 
 
 def ring_buffers(width):
     f32, bf16 = jnp.float32, jnp.bfloat16
-    second = pltpu.VMEM((2, 3, 32, width) if width > 256 else (7, 32, width), bf16)
+    second = pltpu.VMEM((7, 32, width), bf16)
     return [
         pltpu.VMEM((3, 2, 4, 32, width), bf16),
         pltpu.VMEM((3, 2, 4, 32, width), bf16),
@@ -395,11 +383,6 @@
             pltpu.VMEM((2, 3, 4, 8, 128), f32),
             pltpu.VMEM((2, 256, 512), f32),
             [ring_buffers(width) for width in WIDTHS],
-            [
-                pltpu.VMEM((2, 32, 2 * WIDTHS[0]), f32),
-                pltpu.VMEM((32, 2 * WIDTHS[0]), bf16),
-                pltpu.VMEM((32, 2 * WIDTHS[0]), bf16),
-            ],
             pltpu.SemaphoreType.DMA((3,)),
             pltpu.SemaphoreType.DMA((N_SEND,)),
             pltpu.SemaphoreType.DMA((N_RECEIVE,)),

time: 47.8 us -> 46.1 us (0.964)
  Pallas kernels: 47 us -> 45.4 us
    pallas_call x1, Pallas kernels: 47 us -> 45.4 us  [per_device(): pl.pallas_call(kernel, out_shape=pltpu.VMEM((32, D), f32), in_specs=[pl.B...]
where the time goes in v6:
time: 46.1 us
  Pallas kernels  45.4 us (98%)
  local copies, waits for them, and re-layouts  0.68 us (1%)
    pallas_call x1, Pallas kernels, per_device(): pl.pallas_call(kernel, out_shape=pltpu.VMEM((32, D), f32), in_specs=[pl.B...  45.4 us

profile of v6, /device:TPU:0, one launch (start us, length us, event | category | flops | bytes accessed | tf_op | source)
XLA Modules:
  0.0 46.1 jit_solution(15392389581267155829)
XLA Ops:
  0.0 45.4 %shard_map.28 = f32[32,1536]{1,0:T(8,128)S(1)} custom-call(bf16[256,1536]{1,0:T(8,128)(2,1)} %e_hbm.1, bf16[1024,1536]{1,0:T(8,128)(2,1)} %c_hbm.1), custom_call_target="tpu_custom_call" | custom-call | flops 6442450944 | bytes 5242880 | tf_op jit(solution)/shard_map/pallas_call | solution.py:371
  45.4 0.7 %copy.4 = f32[32,1536]{1,0:T(8,128)} copy(f32[32,1536]{1,0:T(8,128)S(1)} %shard_map.28) | data formatting | bytes 393216

commit v7 on v6

--- a/solution.py
+++ b/solution.py
@@ -15,7 +15,7 @@
 ROWS = 256
 SCALE = D**-0.5 * math.log2(math.e)
 SPLIT = (128, 96)
-WIDTHS = (512, 512, 256, 256)
+WIDTHS = (640, 640, 128, 128)
 
 HOME = 0
 NEAR = 2
@@ -381,7 +381,7 @@
             pltpu.VMEM((8, 4 * ROWS), f32),
             pltpu.VMEM((2, 4, 8, 128), f32),
             pltpu.VMEM((2, 3, 4, 8, 128), f32),
-            pltpu.VMEM((2, 256, 512), f32),
+            pltpu.VMEM((2, 256, 640), f32),
             [ring_buffers(width) for width in WIDTHS],
             pltpu.SemaphoreType.DMA((3,)),
             pltpu.SemaphoreType.DMA((N_SEND,)),

time: 46.1 us -> 47.1 us (1.022)
  Pallas kernels: 45.4 us -> 46.1 us
    pallas_call x1, Pallas kernels: 45.4 us -> 46.1 us  [per_device(): pl.pallas_call(kernel, out_shape=pltpu.VMEM((32, D), f32), in_specs=[pl.B...]
where the time goes in v7:
time: 47.1 us; the launch traced here: 46.8 us
  Pallas kernels  46.1 us (98%)
  local copies, waits for them, and re-layouts  0.68 us (1%)
    pallas_call x1, Pallas kernels, per_device(): pl.pallas_call(kernel, out_shape=pltpu.VMEM((32, D), f32), in_specs=[pl.B...  46.1 us

profile of v7, /device:TPU:0, one launch (start us, length us, event | category | flops | bytes accessed | tf_op | source)
XLA Modules:
  0.0 46.8 jit_solution(5588204470385289795)
XLA Ops:
  0.0 46.1 %shard_map.28 = f32[32,1536]{1,0:T(8,128)S(1)} custom-call(bf16[256,1536]{1,0:T(8,128)(2,1)} %e_hbm.1, bf16[1024,1536]{1,0:T(8,128)(2,1)} %c_hbm.1), custom_call_target="tpu_custom_call" | custom-call | flops 6442450944 | bytes 5242880 | tf_op jit(solution)/shard_map/pallas_call | solution.py:371
  46.1 0.7 %copy.4 = f32[32,1536]{1,0:T(8,128)} copy(f32[32,1536]{1,0:T(8,128)S(1)} %shard_map.28) | data formatting | bytes 393216

commit v8 on v6

--- a/solution.py
+++ b/solution.py
@@ -159,9 +159,9 @@
         arrived(outer(j, other), PASSED + j)
         if j == 1:
             arrived(rows.at[pl.ds(6, 2), tail], BOTH)
-        m = dots(2 + j, rows.at[j * 4 + 2], rows.at[j * 4 + 3])
         if j == 0:
             forward(1)
+        m = dots(2 + j, rows.at[j * 4 + 2], rows.at[j * 4 + 3])
         total = exps(2 + j, m)
         note(j, 2, low, m, total)
         note(j, 1, high, m, total)

time: 46.1 us -> 46.2 us (level)
  no operation moved by 1% of the time
where the time goes in v8:
time: 46.2 us; the launch traced here: 46 us
  Pallas kernels  45.3 us (98%)
  local copies, waits for them, and re-layouts  0.68 us (1%)
    pallas_call x1, Pallas kernels, per_device(): pl.pallas_call(kernel, out_shape=pltpu.VMEM((32, D), f32), in_specs=[pl.B...  45.3 us

profile of v8, /device:TPU:0, one launch (start us, length us, event | category | flops | bytes accessed | tf_op | source)
XLA Modules:
  0.0 46.0 jit_solution(8786104078208363053)
XLA Ops:
  0.0 45.3 %shard_map.28 = f32[32,1536]{1,0:T(8,128)S(1)} custom-call(bf16[256,1536]{1,0:T(8,128)(2,1)} %e_hbm.1, bf16[1024,1536]{1,0:T(8,128)(2,1)} %c_hbm.1), custom_call_target="tpu_custom_call" | custom-call | flops 6442450944 | bytes 5242880 | tf_op jit(solution)/shard_map/pallas_call | solution.py:371
  45.3 0.7 %copy.4 = f32[32,1536]{1,0:T(8,128)} copy(f32[32,1536]{1,0:T(8,128)S(1)} %shard_map.28) | data formatting | bytes 393216

commit v9 on v8

--- a/solution.py
+++ b/solution.py
@@ -55,7 +55,7 @@
 
     up, down, far = step(z, 1), step(z, 3), step(z, 2)
     sib = dev(y, x, z, other)
-    partners = [dev(y, x, zz, cc) for zz in (up, down) for cc in (0, 1)] + [sib]
+    partners = [dev(y, x, down, 0), dev(y, x, up, 1), sib]
     partners += [dev(y, step(x, b), z, core) for b in (1, 3)]
     partners += [dev(step(y, b), x, z, core) for b in (1, 3)]
 

time: 46.2 us -> 46 us (level)
  no operation moved by 1% of the time
where the time goes in v9:
time: 46 us; the launch traced here: 45.9 us
  Pallas kernels  45.2 us (98%)
  local copies, waits for them, and re-layouts  0.68 us (1%)
    pallas_call x1, Pallas kernels, per_device(): pl.pallas_call(kernel, out_shape=pltpu.VMEM((32, D), f32), in_specs=[pl.B...  45.2 us

profile of v9, /device:TPU:0, one launch (start us, length us, event | category | flops | bytes accessed | tf_op | source)
XLA Modules:
  0.0 45.9 jit_solution(14599874800583465038)
XLA Ops:
  0.0 45.2 %shard_map.28 = f32[32,1536]{1,0:T(8,128)S(1)} custom-call(bf16[256,1536]{1,0:T(8,128)(2,1)} %e_hbm.1, bf16[1024,1536]{1,0:T(8,128)(2,1)} %c_hbm.1), custom_call_target="tpu_custom_call" | custom-call | flops 6442450944 | bytes 5242880 | tf_op jit(solution)/shard_map/pallas_call | solution.py:371
  45.2 0.7 %copy.4 = f32[32,1536]{1,0:T(8,128)} copy(f32[32,1536]{1,0:T(8,128)S(1)} %shard_map.28) | data formatting | bytes 393216

commit v10 on v9

--- a/solution.py
+++ b/solution.py
@@ -287,7 +287,7 @@
             out_ref[:, self.at : self.at + self.width] = mine + sum(decode(self.rcv2[slot]) for slot in range(2, 7))
 
         def out_straight(self):
-            for across in (1, 0):
+            for across in (0, 1):
                 for by in (2, 1, 3, 0):
                     if by or across:
                         slot = 2 * by + across - 1

time: 46 us -> 46.3 us (level)
  no operation moved by 1% of the time
where the time goes in v10:
time: 46.3 us; the launch traced here: 46.2 us
  Pallas kernels  45.5 us (98%)
  local copies, waits for them, and re-layouts  0.68 us (1%)
    pallas_call x1, Pallas kernels, per_device(): pl.pallas_call(kernel, out_shape=pltpu.VMEM((32, D), f32), in_specs=[pl.B...  45.5 us

profile of v10, /device:TPU:0, one launch (start us, length us, event | category | flops | bytes accessed | tf_op | source)
XLA Modules:
  0.0 46.2 jit_solution(1188226989536141829)
XLA Ops:
  0.0 45.5 %shard_map.28 = f32[32,1536]{1,0:T(8,128)S(1)} custom-call(bf16[256,1536]{1,0:T(8,128)(2,1)} %e_hbm.1, bf16[1024,1536]{1,0:T(8,128)(2,1)} %c_hbm.1), custom_call_target="tpu_custom_call" | custom-call | flops 6442450944 | bytes 5242880 | tf_op jit(solution)/shard_map/pallas_call | solution.py:371
  45.5 0.7 %copy.4 = f32[32,1536]{1,0:T(8,128)} copy(f32[32,1536]{1,0:T(8,128)S(1)} %shard_map.28) | data formatting | bytes 393216
